TPU v7x, 32 devices: a whole 2x2x4 slice. The times are simulated.
32 devices in a mesh: dp: 16 (over z, y, x), mp: 2 (over core).
Axes of the slice: x: 2, y: 2, z: 4, core: 2. Of those that a mesh axis runs over, the one named last changes fastest.
Arguments:
- latents: bfloat16 [8192, 1024], P(('dp', 'mp')), may hold values from -6 to 6
- inputs: bfloat16 [32768, 1024], P(('dp', 'mp')), may hold values from -6 to 6
- valid_counts: int32 [32], P('dp'), may hold values from 1 to 1024, as said below
- cotangent: bfloat16 [8192, 1024], P(('dp', 'mp')), may hold values from -6 to 6
- gain_latent: float32 [1024], replicated, may hold values from 0.1 to 1.9
- shift_latent: float32 [1024], replicated, may hold values from -1.75 to 1.75
- gain_input: float32 [1024], replicated, may hold values from 0.1 to 1.9
- shift_input: float32 [1024], replicated, may hold values from -1.75 to 1.75
- cross_query: bfloat16 [1024, 1024], P(None, 'mp'), may hold values from -0.1875 to 0.1875
- cross_key: bfloat16 [1024, 1024], P(None, 'mp'), may hold values from -0.1875 to 0.1875
- cross_value: bfloat16 [1024, 1024], P(None, 'mp'), may hold values from -0.1875 to 0.1875
- cross_out: bfloat16 [1024, 1024], P('mp'), may hold values from -3 to 3
- gain_self: float32 [1024], replicated, may hold values from 0.1 to 1.9
- shift_self: float32 [1024], replicated, may hold values from -1.75 to 1.75
- self_query: bfloat16 [1024, 1024], P(None, 'mp'), may hold values from -0.1875 to 0.1875
- self_key: bfloat16 [1024, 1024], P(None, 'mp'), may hold values from -0.1875 to 0.1875
- self_value: bfloat16 [1024, 1024], P(None, 'mp'), may hold values from -0.1875 to 0.1875
- self_out: bfloat16 [1024, 1024], P('mp'), may hold values from -3 to 3
- gain_mlp: float32 [1024], replicated, may hold values from 0.1 to 1.9
- shift_mlp: float32 [1024], replicated, may hold values from -1.75 to 1.75
- mlp_in: bfloat16 [1024, 4096], P(None, 'mp'), may hold values from -0.1875 to 0.1875
- mlp_in_bias: float32 [4096], P('mp'), may hold values from -1.75 to 1.75
- mlp_out: bfloat16 [4096, 1024], P('mp'), may hold values from -0.09375 to 0.09375
- mlp_out_bias: float32 [1024], replicated, may hold values from -1.75 to 1.75
Outputs:
- result_latents: bfloat16 [8192, 1024], P(('dp', 'mp'))
- grad_latents: float32 [8192, 1024], P(('dp', 'mp'))
- grad_inputs: float32 [32768, 1024], P(('dp', 'mp'))
- grad_gain_latent: float32 [1024], replicated
- grad_shift_latent: float32 [1024], replicated
- grad_gain_input: float32 [1024], replicated
- grad_shift_input: float32 [1024], replicated
- grad_cross_query: float32 [1024, 1024], P(None, 'mp')
- grad_cross_key: float32 [1024, 1024], P(None, 'mp')
- grad_cross_value: float32 [1024, 1024], P(None, 'mp')
- grad_cross_out: float32 [1024, 1024], P('mp')
- grad_gain_self: float32 [1024], replicated
- grad_shift_self: float32 [1024], replicated
- grad_self_query: float32 [1024, 1024], P(None, 'mp')
- grad_self_key: float32 [1024, 1024], P(None, 'mp')
- grad_self_value: float32 [1024, 1024], P(None, 'mp')
- grad_self_out: float32 [1024, 1024], P('mp')
- grad_gain_mlp: float32 [1024], replicated
- grad_shift_mlp: float32 [1024], replicated
- grad_mlp_in: float32 [1024, 4096], P(None, 'mp')
- grad_mlp_in_bias: float32 [4096], P('mp')
- grad_mlp_out: float32 [4096, 1024], P('mp')
- grad_mlp_out_bias: float32 [1024], replicated
Inputs may be any that keep to these rules, and one draw needn't show every extreme that they name: `valid_counts`: valid inputs of each group are its first ones; each aligned block of 2 groups holds one group with all 1024 inputs valid, and some groups hold only a few.
All inputs are finite; a program needn't handle non-finite values.
Results may differ from a plain program's by a relative error of at most 0.04.
Values may be sent and summed in bfloat16 or wider, within the bound.
A program may use at most 256 MiB of HBM per device.

v0:
```python
from functools import partial

import jax
import jax.numpy as jnp
from jax import lax
from jax.sharding import PartitionSpec as P

HD = 32
GS = 256
IN = 1024


epsilon = 1e-05
negative = -1e30


def layer_norm(stream, norm_gain, norm_shift):
    row_mean = jnp.mean(stream, axis=-1, keepdims=True)
    centered = stream - row_mean
    row_var = jnp.mean(centered * centered, axis=-1, keepdims=True)
    return centered * lax.rsqrt(row_var + epsilon) * norm_gain + norm_shift


def norm_back(stream, norm_gain, norm_shift, upstream):
    outcome, pullback = jax.vjp(layer_norm, stream, norm_gain, norm_shift)
    return pullback(upstream)


def product(left, right):
    return jnp.dot(left, right, preferred_element_type=jnp.float32)


def contract_rows(left, right):
    return lax.dot_general(
        left, right, (((0,), (0,)), ((), ())), preferred_element_type=jnp.float32
    )


def contract_cols(left, right):
    return lax.dot_general(
        left, right, (((1,), (1,)), ((), ())), preferred_element_type=jnp.float32
    )


def score_block(query_blk, key_blk, count_blk, key_limit):
    raw = jnp.einsum("gshe,gkhe->ghsk", query_blk, key_blk, preferred_element_type=jnp.float32)
    scores = raw * HD ** (-0.5)
    positions = jnp.arange(key_limit, dtype=jnp.int32)
    valid_mask = positions[None, :] < count_blk[:, None]
    return jnp.where(valid_mask[:, None, None, :], scores, negative)


def attend_block(operands, key_limit):
    query_blk, key_blk, value_blk, count_blk = operands
    scores = score_block(query_blk, key_blk, count_blk, key_limit)
    top_score = jnp.max(scores, axis=-1, keepdims=True)
    row_total = jnp.sum(jnp.exp(scores - top_score), axis=-1, keepdims=True)
    log_total = top_score + jnp.log(row_total)
    attn_prob = jnp.exp(scores - log_total).astype(jnp.bfloat16)
    mixed = jnp.einsum("ghsk,gkhe->gshe", attn_prob, value_blk, preferred_element_type=jnp.float32)
    return (mixed, log_total[..., 0])


def attend_back(operands, key_limit):
    query_blk, key_blk, value_blk, count_blk, total_blk, grad_blk = operands
    scores = score_block(query_blk, key_blk, count_blk, key_limit)
    attn_full = jnp.exp(scores - total_blk[..., None])
    attn_prob = attn_full.astype(jnp.bfloat16)
    grad_value = jnp.einsum(
        "ghsk,gshe->gkhe", attn_prob, grad_blk, preferred_element_type=jnp.float32
    )
    grad_prob = jnp.einsum(
        "gshe,gkhe->ghsk", grad_blk, value_blk, preferred_element_type=jnp.float32
    )
    inner = jnp.sum(grad_prob * attn_full, axis=-1, keepdims=True)
    grad_score = (attn_full * (grad_prob - inner) * HD ** (-0.5)).astype(jnp.bfloat16)
    grad_query = jnp.einsum(
        "ghsk,gkhe->gshe", grad_score, key_blk, preferred_element_type=jnp.float32
    )
    grad_key = jnp.einsum(
        "ghsk,gshe->gkhe", grad_score, query_blk, preferred_element_type=jnp.float32
    )
    return (grad_query, grad_key, grad_value)


def pair_apply(block_fn, span, operands):
    return block_fn(operands, key_limit=span)


def group_size_of():
    return 2


def attention_forward(queries, key_rows, value_rows, counts, span):
    group_count = counts.shape[0]
    pair_size = group_size_of()
    pair_count = group_count // pair_size
    head_local = queries.shape[1] // HD
    query_pairs = queries.reshape(pair_count, pair_size, GS, head_local, HD)
    key_pairs = key_rows.reshape(pair_count, pair_size, span, head_local, HD)
    value_pairs = value_rows.reshape(pair_count, pair_size, span, head_local, HD)
    count_pairs = counts.reshape(pair_count, pair_size)

    def one_pair(pieces):
        return pair_apply(attend_block, span, pieces)

    mixed, log_total = lax.map(one_pair, (query_pairs, key_pairs, value_pairs, count_pairs))
    return (mixed.reshape(group_count * GS, head_local * HD).astype(jnp.bfloat16), log_total)


def attention_backward(queries, key_rows, value_rows, counts, log_total, grad_mixed, span):
    group_count = counts.shape[0]
    pair_size = group_size_of()
    pair_count = group_count // pair_size
    head_local = queries.shape[1] // HD
    query_pairs = queries.reshape(pair_count, pair_size, GS, head_local, HD)
    key_pairs = key_rows.reshape(pair_count, pair_size, span, head_local, HD)
    value_pairs = value_rows.reshape(pair_count, pair_size, span, head_local, HD)
    count_pairs = counts.reshape(pair_count, pair_size)
    grad_pairs = grad_mixed.reshape(pair_count, pair_size, GS, head_local, HD)

    def one_pair(pieces):
        return pair_apply(attend_back, span, pieces)

    grad_query, grad_key, grad_value = lax.map(
        one_pair, (query_pairs, key_pairs, value_pairs, count_pairs, log_total, grad_pairs)
    )
    width_local = head_local * HD
    return (
        grad_query.reshape(group_count * GS, width_local).astype(jnp.bfloat16),
        grad_key.reshape(group_count * span, width_local).astype(jnp.bfloat16),
        grad_value.reshape(group_count * span, width_local).astype(jnp.bfloat16),
    )


def local(
    latents,
    inputs,
    valid_counts,
    cotangent,
    gain_latent,
    shift_latent,
    gain_input,
    shift_input,
    cross_query,
    cross_key,
    cross_value,
    cross_out,
    gain_self,
    shift_self,
    self_query,
    self_key,
    self_value,
    self_out,
    gain_mlp,
    shift_mlp,
    mlp_in,
    mlp_in_bias,
    mlp_out,
    mlp_out_bias,
):
    stream_zero = latents.astype(jnp.float32)
    input_rows = inputs.astype(jnp.float32)
    latent_normed = layer_norm(stream_zero, gain_latent, shift_latent).astype(jnp.bfloat16)
    input_normed = layer_norm(input_rows, gain_input, shift_input).astype(jnp.bfloat16)
    cross_rows, cross_inputs, all_cotangent = (
        lax.all_gather(latent_normed, "mp", axis=0, tiled=True),
        lax.all_gather(input_normed, "mp", axis=0, tiled=True),
        lax.all_gather(cotangent, "mp", axis=0, tiled=True),
    )
    cross_queries = product(cross_rows, cross_query).astype(jnp.bfloat16)
    cross_keys = product(cross_inputs, cross_key).astype(jnp.bfloat16)
    cross_values = product(cross_inputs, cross_value).astype(jnp.bfloat16)
    cross_mixed, cross_total = attention_forward(
        cross_queries, cross_keys, cross_values, valid_counts, IN
    )
    stream_one = stream_zero + lax.psum_scatter(
        product(cross_mixed, cross_out).astype(jnp.bfloat16), "mp", scatter_dimension=0, tiled=True
    ).astype(jnp.float32)
    self_normed = layer_norm(stream_one, gain_self, shift_self).astype(jnp.bfloat16)
    self_rows = lax.all_gather(self_normed, "mp", axis=0, tiled=True)
    self_queries = product(self_rows, self_query).astype(jnp.bfloat16)
    self_keys = product(self_rows, self_key).astype(jnp.bfloat16)
    self_values = product(self_rows, self_value).astype(jnp.bfloat16)
    full_counts = jnp.full(valid_counts.shape, GS, jnp.int32)
    self_mixed, self_total = attention_forward(
        self_queries, self_keys, self_values, full_counts, GS
    )
    stream_two = stream_one + lax.psum_scatter(
        product(self_mixed, self_out).astype(jnp.bfloat16), "mp", scatter_dimension=0, tiled=True
    ).astype(jnp.float32)
    mlp_normed = layer_norm(stream_two, gain_mlp, shift_mlp).astype(jnp.bfloat16)
    mlp_rows = lax.all_gather(mlp_normed, "mp", axis=0, tiled=True)
    hidden = product(mlp_rows, mlp_in) + mlp_in_bias
    activation = jax.nn.gelu(hidden, approximate=False).astype(jnp.bfloat16)
    stream_three = stream_two + (
        lax.psum_scatter(
            product(activation, mlp_out).astype(jnp.bfloat16), "mp", scatter_dimension=0, tiled=True
        ).astype(jnp.float32)
        + mlp_out_bias
    )
    result_latents = stream_three.astype(jnp.bfloat16)
    grad_mlp_out = contract_rows(activation, all_cotangent)
    grad_mlp_out_bias = jnp.sum(all_cotangent, axis=0, dtype=jnp.float32)
    grad_activation = contract_cols(all_cotangent, mlp_out)
    outcome, gelu_pull = jax.vjp(partial(jax.nn.gelu, approximate=False), hidden)
    grad_hidden = gelu_pull(grad_activation)[0].astype(jnp.bfloat16)
    grad_mlp_in = contract_rows(mlp_rows, grad_hidden)
    grad_mlp_in_bias = jnp.sum(grad_hidden, axis=0, dtype=jnp.float32)
    grad_mlp_normed = lax.psum_scatter(
        contract_cols(grad_hidden, mlp_in).astype(jnp.bfloat16),
        "mp",
        scatter_dimension=0,
        tiled=True,
    ).astype(jnp.float32)
    grad_added, grad_gain_mlp, grad_shift_mlp = norm_back(
        stream_two, gain_mlp, shift_mlp, grad_mlp_normed
    )
    grad_two = cotangent.astype(jnp.float32) + grad_added
    self_cotangent = lax.all_gather(grad_two.astype(jnp.bfloat16), "mp", axis=0, tiled=True)
    grad_self_out = contract_rows(self_mixed, self_cotangent)
    grad_self_mixed = contract_cols(self_cotangent, self_out).astype(jnp.bfloat16)
    grad_self_queries, grad_self_keys, grad_self_values = attention_backward(
        self_queries, self_keys, self_values, full_counts, self_total, grad_self_mixed, GS
    )
    grad_self_query = contract_rows(self_rows, grad_self_queries)
    grad_self_key = contract_rows(self_rows, grad_self_keys)
    grad_self_value = contract_rows(self_rows, grad_self_values)
    grad_self_normed = lax.psum_scatter(
        (
            contract_cols(grad_self_queries, self_query)
            + contract_cols(grad_self_keys, self_key)
            + contract_cols(grad_self_values, self_value)
        ).astype(jnp.bfloat16),
        "mp",
        scatter_dimension=0,
        tiled=True,
    ).astype(jnp.float32)
    grad_added, grad_gain_self, grad_shift_self = norm_back(
        stream_one, gain_self, shift_self, grad_self_normed
    )
    grad_one = grad_two + grad_added
    cross_cotangent = lax.all_gather(grad_one.astype(jnp.bfloat16), "mp", axis=0, tiled=True)
    grad_cross_out = contract_rows(cross_mixed, cross_cotangent)
    grad_cross_mixed = contract_cols(cross_cotangent, cross_out).astype(jnp.bfloat16)
    grad_cross_queries, grad_cross_keys, grad_cross_values = attention_backward(
        cross_queries, cross_keys, cross_values, valid_counts, cross_total, grad_cross_mixed, IN
    )
    grad_cross_query = contract_rows(cross_rows, grad_cross_queries)
    grad_cross_key = contract_rows(cross_inputs, grad_cross_keys)
    grad_cross_value = contract_rows(cross_inputs, grad_cross_values)
    latent_part = contract_cols(grad_cross_queries, cross_query)
    input_part = contract_cols(grad_cross_keys, cross_key) + contract_cols(
        grad_cross_values, cross_value
    )
    grad_latent_normed, grad_input_normed = (
        lax.psum_scatter(
            latent_part.astype(jnp.bfloat16), "mp", scatter_dimension=0, tiled=True
        ).astype(jnp.float32),
        lax.psum_scatter(
            input_part.astype(jnp.bfloat16), "mp", scatter_dimension=0, tiled=True
        ).astype(jnp.float32),
    )
    grad_added, grad_gain_latent, grad_shift_latent = norm_back(
        stream_zero, gain_latent, shift_latent, grad_latent_normed
    )
    grad_latents = grad_one + grad_added
    grad_inputs, grad_gain_input, grad_shift_input = norm_back(
        input_rows, gain_input, shift_input, grad_input_normed
    )
    (
        grad_gain_latent,
        grad_shift_latent,
        grad_gain_input,
        grad_shift_input,
        grad_gain_self,
        grad_shift_self,
        grad_gain_mlp,
        grad_shift_mlp,
    ) = lax.psum(
        (
            grad_gain_latent,
            grad_shift_latent,
            grad_gain_input,
            grad_shift_input,
            grad_gain_self,
            grad_shift_self,
            grad_gain_mlp,
            grad_shift_mlp,
        ),
        ("dp", "mp"),
    )
    (
        grad_cross_query,
        grad_cross_key,
        grad_cross_value,
        grad_cross_out,
        grad_self_query,
        grad_self_key,
        grad_self_value,
        grad_self_out,
        grad_mlp_in,
        grad_mlp_in_bias,
        grad_mlp_out,
        grad_mlp_out_bias,
    ) = lax.psum(
        (
            grad_cross_query,
            grad_cross_key,
            grad_cross_value,
            grad_cross_out,
            grad_self_query,
            grad_self_key,
            grad_self_value,
            grad_self_out,
            grad_mlp_in,
            grad_mlp_in_bias,
            grad_mlp_out,
            grad_mlp_out_bias,
        ),
        "dp",
    )
    return (
        result_latents,
        grad_latents,
        grad_inputs,
        grad_gain_latent,
        grad_shift_latent,
        grad_gain_input,
        grad_shift_input,
        grad_cross_query,
        grad_cross_key,
        grad_cross_value,
        grad_cross_out,
        grad_gain_self,
        grad_shift_self,
        grad_self_query,
        grad_self_key,
        grad_self_value,
        grad_self_out,
        grad_gain_mlp,
        grad_shift_mlp,
        grad_mlp_in,
        grad_mlp_in_bias,
        grad_mlp_out,
        grad_mlp_out_bias,
    )


def solution(mesh):
    return jax.shard_map(
        local,
        mesh=mesh,
        in_specs=(
            P(("dp", "mp"), None),
            P(("dp", "mp"), None),
            P("dp"),
            P(("dp", "mp"), None),
            P(),
            P(),
            P(),
            P(),
            P(None, "mp"),
            P(None, "mp"),
            P(None, "mp"),
            P("mp", None),
            P(),
            P(),
            P(None, "mp"),
            P(None, "mp"),
            P(None, "mp"),
            P("mp", None),
            P(),
            P(),
            P(None, "mp"),
            P("mp"),
            P("mp", None),
            P(),
        ),
        out_specs=(
            P(("dp", "mp"), None),
            P(("dp", "mp"), None),
            P(("dp", "mp"), None),
            P(),
            P(),
            P(),
            P(),
            P(None, "mp"),
            P(None, "mp"),
            P(None, "mp"),
            P("mp", None),
            P(),
            P(),
            P(None, "mp"),
            P(None, "mp"),
            P(None, "mp"),
            P("mp", None),
            P(),
            P(),
            P(None, "mp"),
            P("mp"),
            P("mp", None),
            P(),
        ),
        check_vma=False,
    )
```

profile of v0, /device:TPU:0, one launch (start us, length us, event | category | flops | bytes accessed | tf_op | source)
XLA Modules:
  0.0 1500.3 jit_solution(6734078875233386547)
XLA Ops:
  19.0 4.9 all-gather.10.cloned.1.call-done
  26.3 14.7 all-gather.8.cloned.1.call-done
  41.0 6.1 convolution_convert_fusion.1
  55.6 5.8 convolution_convert_fusion
  69.9 15.5 %fusion.5 = (f32[2,16,256]{2,1,0:T(8,128)S(1)}, f32[2,16,256,1024]{3,2,1,0:T(8,128)}) fusion(pred[2,1024]{1,0:T(4,128)(4,1)S(1)} %iota_compare_fusion, bf16[2,1024,16,32]{1,0,3,2:T(2,128)(2,1)} %squeeze.66, bf16[2,256,16,32]{1,0,3,2:T(2,128)(2,1)S(1)} %squeeze.65), kind=kOutput, calls=%fused_computation.8 | convolution fusion | flops 562028544 | bytes 36210688 | tf_op jit(solution)/shard_map/while/body/eval_jaxpr/gshe,gkhe->ghsk/dot_general | solution.py:46
  85.4 14.7 exponential_reduce_fusion
  100.1 15.4 %fusion.117 = bf16[2,256,16,32]{1,3,2,0:T(8,128)(2,1)S(1)} fusion(bf16[2,1024,16,32]{1,0,3,2:T(2,128)(2,1)} %squeeze.64, f32[2,16,256,1024]{3,2,1,0:T(8,128)} %get-tuple-element.165, f32[2,16,256]{2,1,0:T(8,128)S(1)} %log_add_fusion.1, pred[2,1024]{1,0:T(4,128)(4,1)S(1)} %iota_compare_fusion), kind=kOutput, calls=%fused_computation.134 | convolution fusion | flops 570687488 | bytes 36210688 | tf_op jit(solution)/shard_map/while/body/eval_jaxpr/ghsk,gkhe->gshe/dot_general | solution.py:60
  118.8 9.8 reduce-scatter.8.cloned.1.call-done
  133.5 10.3 all-gather.12.cloned.1.call-done
  171.2 9.8 reduce-scatter.10.cloned.1.call-done
  184.7 9.4 all-gather.14.cloned.1.call-done
  194.0 6.9 fusion.189
  200.9 4.9 all-gather.16.cloned.1.call-done
  205.8 16.5 %convert_reduce_fusion.2 = (f32[2048]{0:T(1024)}, bf16[512,2048]{1,0:T(8,128)(2,1)S(1)}, f32[512,2048]{1,0:T(8,128)}) fusion(f32[512,2048]{1,0:T(8,128)} %fusion.189, f32[2048]{0:T(1024)S(1)} %copy-done.68, bf16[512,1024]{1,0:T(8,128)(2,1)} %all-gather.16.cloned.1.call-done, bf16[2048,1024]{1,0:T(8,128)(2,1)} %param.46), kind=kOutput, calls=%fused_computation.49 | convolution fusion | flops 2226124800 | bytes 15745024 | tf_op jit(solution)/shard_map/dot_general | solution.py:40
  227.0 4.6 multiply_convert_fusion.2
  238.3 11.2 reduce-scatter.12.cloned.1.call-done
  255.0 10.3 all-gather.18.cloned.1.call-done
  269.8 4.7 fusion.137
  274.5 14.5 fusion.107
  289.0 16.3 %fusion.104 = bf16[2,256,16,32]{1,3,2,0:T(8,128)(2,1)} fusion(f32[2,16,256,256]{2,3,1,0:T(8,128)} %fusion.137, f32[2,16,256,256]{2,3,1,0:T(8,128)} %copy-done.3, f32[2,16,256]{2,1,0:T(8,128)S(1)} %log_add_fusion, pred[2,256]{1,0:T(4,128)(4,1)S(1)} %iota_compare_fusion.1, bf16[2,256,16,32]{1,0,3,2:T(2,128)(2,1)S(1)} %copy-done.40), kind=kOutput, calls=%fused_computation.129 | convolution fusion | flops 157556992 | bytes 17859072 | tf_op jit(solution)/shard_map/while/body/eval_jaxpr/ghsk,gshe->gkhe/dot_general | solution.py:80
  305.3 5.3 fusion.111
  317.0 9.6 reduce-scatter.16.cloned.1.call-done
  332.8 10.3 all-gather.20.cloned.1.call-done
  345.7 14.7 fusion.74
  360.4 54.7 %fusion.112 = bf16[2,256,16,32]{1,3,2,0:T(8,128)(2,1)S(1)} fusion(f32[2,16,256,1024]{3,2,1,0:T(8,128)} %fusion.74, f32[2,16,256,1024]{3,2,1,0:T(8,128)} %get-tuple-element.165, f32[2,16,256]{2,1,0:T(8,128)S(1)} %log_add_fusion.1, pred[2,1024]{1,0:T(4,128)(4,1)S(1)} %iota_compare_fusion, bf16[2,1024,16,32]{1,0,3,2:T(2,128)(2,1)} %squeeze.66), kind=kOutput, calls=%fused_computation.133 | convolution fusion | flops 629416960 | bytes 69765120 | tf_op jit(solution)/shard_map/while/body/eval_jaxpr/ghsk,gkhe->gshe/dot_general | solution.py:77
  418.8 15.8 %convert_bitcast_fusion = bf16[2,1024,16,32]{1,3,2,0:T(8,128)(2,1)} fusion(bf16[2,256,16,32]{1,0,3,2:T(2,128)(2,1)S(1)} %squeeze.71, f32[2,16,256,1024]{3,2,1,0:T(8,128)} %get-tuple-element.165, f32[2,16,256]{2,1,0:T(8,128)S(1)} %log_add_fusion.1, pred[2,1024]{1,0:T(4,128)(4,1)S(1)} %iota_compare_fusion), kind=kOutput, calls=%fused_computation.78 | convolution fusion | flops 571473920 | bytes 36210688 | tf_op jit(solution)/shard_map/while/body/eval_jaxpr/ghsk,gshe->gkhe/dot_general | solution.py:69
  434.7 69.6 %convert_bitcast_fusion.1 = bf16[2,1024,16,32]{1,3,2,0:T(8,128)(2,1)} fusion(f32[2,16,256,1024]{3,2,1,0:T(8,128)} %fusion.74, f32[2,16,256,1024]{3,2,1,0:T(8,128)} %get-tuple-element.165, f32[2,16,256]{2,1,0:T(8,128)S(1)} %log_add_fusion.1, pred[2,1024]{1,0:T(4,128)(4,1)S(1)} %iota_compare_fusion, bf16[2,256,16,32]{1,0,3,2:T(2,128)(2,1)S(1)} %copy-done.18), kind=kOutput, calls=%fused_computation.79 | convolution fusion | flops 630203392 | bytes 69765120 | tf_op jit(solution)/shard_map/while/body/eval_jaxpr/ghsk,gshe->gkhe/dot_general | solution.py:80
  518.8 7.9 fusion.201
  526.8 5.8 fusion.202
  554.3 80.9 %all-reduce.1 = (f32[2048]{0:T(1024)}, f32[1024]{0:T(1024)}) all-reduce(f32[2048]{0:T(1024)S(1)} %copy-done.67, f32[1024]{0:T(1024)S(1)} %convert_reduce_fusion.3), channel_id=1, replica_groups=mesh['dp'=16,'mp'=2] {'dp'}, use_global_device_ids=true, to_apply=%region_55.56 | all-reduce | flops 3072 | bytes 24576 | tf_op jit(solution)/shard_map/psum | solution.py:306
  649.1 41.6 %all-reduce = (f32[1024]{0:T(1024)}, f32[1024]{0:T(1024)}, f32[1024]{0:T(1024)}, f32[1024]{0:T(1024)}, f32[1024]{0:T(1024)}, /*index=5*/f32[1024]{0:T(1024)}, f32[1024]{0:T(1024)}, f32[1024]{0:T(1024)}) all-reduce(f32[1024]{0:T(1024)S(1)} %get-tuple-element.117, ...), channel_id=1, replica_groups=mesh['dp'=16,'mp'=2] {'dp','mp'}, use_global_device_ids=true, to_apply=%region_30.31 | all-reduce | flops 8192 | bytes 65536 | tf_op jit(solution)/shard_map/psum | solution.py:280
  695.2 774.3 %all-reduce.5.cloned.1.call-done = (f32[1024,512]{1,0:T(8,128)}, f32[1024,512]{1,0:T(8,128)}, f32[1024,512]{1,0:T(8,128)}, f32[512,1024]{1,0:T(8,128)}, f32[1024...) async-done(((f32[1024,512]{1,0:T(8,128)}, f32[1024,512]{1,0:T(8,128)}, ...) | async-done | bytes 33554448 | tf_op jit(solution)/shard_map/psum | solution.py:306
  (321 shorter events, 188.1 us)
Async XLA Ops:
  7.2 48.4 %copy-start = (bf16[1024,512]{1,0:T(8,128)(2,1)S(1)}, bf16[1024,512]{1,0:T(8,128)(2,1)}, u32[]{:S(2)}) copy-start(bf16[1024,512]{1,0:T(8,128)(2,1)} %param.33) | copy-start | bytes 3145732
  7.2 16.7 %all-gather.10.cloned.1.call-start = ((), (), s32[]{:S(2)}) async-start(), calls=%async_computation.8 | async-start | bytes 1572864 | tf_op jit(solution)/shard_map/all_gather | solution.py:167
  12.1 28.9 %all-gather.8.cloned.1.call-start = ((), (), s32[]{:S(2)}) async-start(), calls=%async_computation.7 | async-start | bytes 6291456 | tf_op jit(solution)/shard_map/all_gather | solution.py:168
  18.9 109.7 %reduce-scatter.8.cloned.1.call-start = ((), (), s32[]{:S(2)}) async-start(), calls=%async_computation.9 | async-start | bytes 1572864 | tf_op jit(solution)/shard_map/reduce_scatter | solution.py:177
  26.2 43.6 %copy-start.17 = (bf16[2,256,16,32]{1,0,3,2:T(2,128)(2,1)}, bf16[2,256,16,32]{1,0,3,2:T(2,128)(2,1)S(1)}, u32[]{:S(2)}) copy-start(bf16[2,256,16,32]{1,0,3,2:T(2,128)(2,1)S(1)} %squeeze.65) | copy-start | bytes 1572868
  100.1 16.9 %copy-start.78 = (bf16[512,1024]{1,0:T(8,128)(2,1)S(1)}, bf16[512,1024]{1,0:T(8,128)(2,1)}, u32[]{:S(2)}) copy-start(bf16[512,1024]{1,0:T(8,128)(2,1)} %param.35) | copy-start | bytes 3145732
  115.6 15.7 %copy-start.53 = (f32[1024]{0:T(1024)S(1)}, f32[1024]{0:T(1024)}, u32[]{:S(2)}) copy-start(f32[1024]{0:T(1024)} %param.36) | copy-start | bytes 12292
  118.8 25.0 %all-gather.12.cloned.1.call-start = ((), (), s32[]{:S(2)}) async-start(), calls=%async_computation.10 | async-start | bytes 1572864 | tf_op jit(solution)/shard_map/all_gather | solution.py:181
  133.4 47.6 %reduce-scatter.10.cloned.1.call-start = ((), (), s32[]{:S(2)}) async-start(), calls=%async_computation.11 | async-start | bytes 1572864 | tf_op jit(solution)/shard_map/reduce_scatter | solution.py:189
  148.3 16.4 %copy-start.23 = (bf16[2,256,16,32]{1,0,3,2:T(2,128)(2,1)}, bf16[2,256,16,32]{1,0,3,2:T(2,128)(2,1)S(1)}, u32[]{:S(2)}) copy-start(bf16[2,256,16,32]{1,0,3,2:T(2,128)(2,1)S(1)} %squeeze.67) | copy-start | bytes 1572868
  171.1 22.9 %all-gather.14.cloned.1.call-start = ((), (), s32[]{:S(2)}) async-start(), calls=%async_computation.12 | async-start | bytes 1572864 | tf_op jit(solution)/shard_map/all_gather | solution.py:193
  183.7 22.1 %all-gather.16.cloned.1.call-start = ((), (), s32[]{:S(2)}) async-start(), calls=%async_computation.14 | async-start | bytes 1572864 | tf_op jit(solution)/shard_map/all_gather | solution.py:169
  184.4 21.4 %copy-start.68 = (f32[2048]{0:T(1024)S(1)}, f32[2048]{0:T(1024)}, u32[]{:S(2)}) copy-start(f32[2048]{0:T(1024)} %param.45) | copy-start | bytes 24580
  184.4 52.4 %reduce-scatter.14.cloned.1.call-start = ((), (), s32[]{:S(2)}) async-start(), calls=%async_computation.15 | async-start | bytes 1572864 | tf_op jit(solution)/shard_map/reduce_scatter | solution.py:210
  205.8 17.8 %copy-start.74 = (bf16[1024,2048]{1,0:T(8,128)(2,1)S(1)}, bf16[1024,2048]{1,0:T(8,128)(2,1)}, u32[]{:S(2)}) copy-start(bf16[1024,2048]{1,0:T(8,128)(2,1)} %param.44) | copy-start | bytes 12582916
  227.0 22.5 %reduce-scatter.12.cloned.1.call-start = ((), (), s32[]{:S(2)}) async-start(), calls=%async_computation.13 | async-start | bytes 1572864 | tf_op jit(solution)/shard_map/reduce_scatter | solution.py:197
  233.0 16.5 %copy-start.72 = (f32[1024]{0:T(1024)S(1)}, f32[1024]{0:T(1024)}, u32[]{:S(2)}) copy-start(f32[1024]{0:T(1024)} %param.47) | copy-start | bytes 12292
  236.3 28.9 %all-gather.18.cloned.1.call-start = ((), (), s32[]{:S(2)}) async-start(), calls=%async_computation.16 | async-start | bytes 1572864 | tf_op jit(solution)/shard_map/all_gather | solution.py:220
  251.9 17.8 %copy-start.24 = (bf16[2,256,16,32]{1,0,3,2:T(2,128)(2,1)S(1)}, bf16[2,256,16,32]{1,0,3,2:T(2,128)(2,1)}, u32[]{:S(2)}) copy-start(bf16[2,256,16,32]{1,0,3,2:T(2,128)(2,1)} %copy-done.23) | copy-start | bytes 1572868
  254.9 71.7 %reduce-scatter.16.cloned.1.call-start = ((), (), s32[]{:S(2)}) async-start(), calls=%async_computation.17 | async-start | bytes 1572864 | tf_op jit(solution)/shard_map/reduce_scatter | solution.py:229
  316.8 26.3 %all-gather.20.cloned.1.call-start = ((), (), s32[]{:S(2)}) async-start(), calls=%async_computation.18 | async-start | bytes 1572864 | tf_op jit(solution)/shard_map/all_gather | solution.py:243
  332.8 302.4 %reduce-scatter.18.cloned.1.call-start = ((), (), s32[]{:S(2)}) async-start(), calls=%async_computation.19 | async-start | bytes 1572864 | tf_op jit(solution)/shard_map/reduce_scatter | solution.py:257
  418.7 15.9 %copy-start.18 = (bf16[2,256,16,32]{1,0,3,2:T(2,128)(2,1)S(1)}, bf16[2,256,16,32]{1,0,3,2:T(2,128)(2,1)}, u32[]{:S(2)}) copy-start(bf16[2,256,16,32]{1,0,3,2:T(2,128)(2,1)} %copy-done.17) | copy-start | bytes 1572868
  418.8 222.1 %reduce-scatter.20.cloned.1.call-start = ((), (), s32[]{:S(2)}) async-start(), calls=%async_computation.20 | async-start | bytes 6291456 | tf_op jit(solution)/shard_map/reduce_scatter | solution.py:260
  518.6 950.9 %all-reduce.5.cloned.1.call-start = ((), (), s32[]{:S(2)}) async-start(), calls=%async_computation.21 | async-start | bytes 67108864 | tf_op jit(solution)/shard_map/psum | solution.py:306
  552.7 82.5 %copy-start.52 = (f32[1024]{0:T(1024)S(1)}, f32[1024]{0:T(1024)}, u32[]{:S(2)}) copy-start(f32[1024]{0:T(1024)} %param.28) | copy-start | bytes 12292
  552.7 82.5 %copy-start.62 = (f32[256]{0:T(256)S(1)}, f32[256]{0:T(256)}, u32[]{:S(2)}) copy-start(f32[256]{0:T(256)} %copy-done.61) | copy-start | bytes 3076
  552.7 84.0 %copy-start.66 = (f32[256]{0:T(256)S(1)}, f32[256]{0:T(256)}, u32[]{:S(2)}) copy-start(f32[256]{0:T(256)} %copy-done.65) | copy-start | bytes 3076
  552.7 84.0 %copy-start.64 = (f32[256]{0:T(256)S(1)}, f32[256]{0:T(256)}, u32[]{:S(2)}) copy-start(f32[256]{0:T(256)} %copy-done.63) | copy-start | bytes 3076
  552.7 85.7 %copy-start.16 = (f32[256,1024]{1,0:T(8,128)S(1)}, f32[256,1024]{1,0:T(8,128)}, u32[]{:S(2)}) copy-start(f32[256,1024]{1,0:T(8,128)} %get-tuple-element.158) | copy-start | bytes 3145732
  552.7 88.2 %copy-start.51 = (f32[1024]{0:T(1024)S(1)}, f32[1024]{0:T(1024)}, u32[]{:S(2)}) copy-start(f32[1024]{0:T(1024)} %copy-done.50) | copy-start | bytes 12292
  552.7 88.2 %copy-start.57 = (f32[1024]{0:T(1024)S(1)}, f32[1024]{0:T(1024)}, u32[]{:S(2)}) copy-start(f32[1024]{0:T(1024)} %param.30) | copy-start | bytes 12292
  (69 other events, 358.5 us)
Sparse Core Ops, SparseCore 0:
  12.2 11.7 all-gather.9
  26.1 14.8 all-gather.7
  118.9 9.6 reduce-scatter.7
  133.5 10.1 all-gather.11
  171.2 9.6 reduce-scatter.9
  183.8 10.1 all-gather.13
  195.6 10.1 all-gather.15
  227.1 9.6 reduce-scatter.13
  239.7 9.6 reduce-scatter.11
  255.1 10.1 all-gather.17
  316.9 9.6 reduce-scatter.15
  332.9 10.1 all-gather.19
  418.9 9.6 reduce-scatter.17
  518.7 13.2 reduce-scatter.19
  552.8 916.6 all-reduce.4
where the time goes:
time: 1510 us; the launch traced here: 1500 us
  waiting for transfers between devices  881 us (58%)
  matrix products  338 us (22%)
  blocking collectives  123 us (8%)
  other arithmetic  72 us (5%)
  local copies, waits for them, and re-layouts  70.1 us (5%)
  between operations  15.3 us (1%)
    psum x1, waiting for transfers between devices, local(): lax.psum((grad_cross_query, grad_cross_key, grad_cross_value, grad_cross_...  774 us
    dot_general x2, matrix products, attend_back(): jnp.einsum('ghsk,gshe->gkhe', grad_score, query_blk, preferred_element_ty...  85.9 us
    psum x1, blocking collectives, local(): lax.psum((grad_cross_query, grad_cross_key, grad_cross_value, grad_cross_...  80.9 us
    dot_general x2, matrix products, attend_back(): jnp.einsum('ghsk,gkhe->gshe', grad_score, key_blk, preferred_element_type...  69.2 us
    psum x1, blocking collectives, local(): lax.psum((grad_gain_latent, grad_shift_latent, grad_gain_input, grad_shif...  41.6 us
    dot_general x10, matrix products, contract_cols(): lax.dot_general(left, right, (((1,), (1,)), ((), ())), preferred_element_...  37.6 us
    dot_general x10, matrix products, product(): return jnp.dot(left, right, preferred_element_type=jnp.float32)  35.5 us
    dot_general x10, matrix products, contract_rows(): lax.dot_general(left, right, (((0,), (0,)), ((), ())), preferred_element_...  33.7 us
  transfers between devices with their start and end apart: 15, of which 13 were waited for; matrix products, arithmetic and copies ran while one was open for 12% of the time, Pallas kernels for 0%

commit v1 on v0

--- a/solution.py
+++ b/solution.py
@@ -1,13 +1,371 @@
+import functools
 from functools import partial
 
 import jax
 import jax.numpy as jnp
 from jax import lax
+from jax.experimental import pallas as pl
+from jax.experimental.pallas import tpu as pltpu
 from jax.sharding import PartitionSpec as P
 
 HD = 32
 GS = 256
 IN = 1024
+
+
+MESH = pl.DeviceIdType.MESH
+NS = 16
+AHEAD = 2
+ORDER = (("a", -2), ("b", 0), ("f", 2), ("j", 4), ("d", 1), ("h", 3), ("c", 0), ("g", 2), ("e", 1), ("i", 3), ("k", 6))
+CH = 256
+HALF = CH // 2
+PIECE = HALF // 4
+SUB = PIECE // 2
+SMALL = 16
+
+
+def reduce_kernel(pairs, g_ref, small_ref, out_ref, small_out, own, xr, ur, dr, fb, yr, sacc, sbuf, send, recv, loc, ssend, srecv):
+    dp = lax.axis_index("dp")
+    core = lax.axis_index("mp")
+    z = dp // 4
+    px = lax.rem(dp, 2)
+    py = lax.rem(dp // 2, 2)
+    x_dev = (dp + 1 - 2 * px, core)
+    y_dev = (dp + 2 - 4 * py, core)
+    c_dev = (dp, 1 - core)
+    up_dev = (dp + 4, core)
+    down_dev = (dp - 4, core)
+    z1_dev = (dp + 4 - 8 * lax.rem(z, 2), core)
+    z2_dev = (dp + 8 - 16 * (z // 2), core)
+    has_up = z < 3
+    has_down = z > 0
+
+    barrier = pltpu.get_barrier_semaphore()
+    for dev in (x_dev, y_dev, c_dev, z2_dev):
+        pl.semaphore_signal(barrier, inc=1, device_id=dev, device_id_type=MESH)
+
+    @pl.when(has_up)
+    def _():
+        pl.semaphore_signal(barrier, inc=1, device_id=up_dev, device_id_type=MESH)
+
+    @pl.when(has_down)
+    def _():
+        pl.semaphore_signal(barrier, inc=1, device_id=down_dev, device_id_type=MESH)
+
+    pl.semaphore_wait(barrier, 4 + has_up.astype(jnp.int32) + has_down.astype(jnp.int32))
+
+    def remote(src, dst, kind, p, s, dev):
+        slot = lax.rem(p, NS)
+        return pltpu.make_async_remote_copy(
+            src_ref=src, dst_ref=dst, send_sem=send.at[kind, s, slot], recv_sem=recv.at[kind, s, slot],
+            device_id=dev, device_id_type=MESH)
+
+    a_pos = (px, py)
+    b_pos = (py, px)
+    a_dev = (x_dev, y_dev)
+    b_dev = (y_dev, x_dev)
+
+    def base(p, s):
+        return (2 * p + s) * CH
+
+    def first(p, s):
+        c = 2 * p + s
+        return remote(g_ref.at[pl.ds(base(p, s) + (1 - a_pos[s]) * HALF, HALF)], xr.at[c], 0, p, s, a_dev[s])
+
+    def mine(p, s):
+        c = 2 * p + s
+        return pltpu.make_async_copy(g_ref.at[pl.ds(base(p, s) + a_pos[s] * HALF, HALF)], own.at[c], loc.at[0, s, lax.rem(p, NS)])
+
+    def up(p, s, lo):
+        c = 2 * p + s
+        src = xr if lo == 1 else ur
+        return remote(src.at[c, pl.ds(lo * PIECE, (4 - lo) * PIECE)], ur.at[c, pl.ds(lo * PIECE, (4 - lo) * PIECE)], 1, p, s, up_dev)
+
+    def down(p, s, hi):
+        c = 2 * p + s
+        src = xr if hi == 3 else dr
+        return remote(src.at[c, pl.ds(0, hi * PIECE)], dr.at[c, pl.ds(0, hi * PIECE)], 2, p, s, down_dev)
+
+    def last(p, s):
+        c = 2 * p + s
+        return remote(fb.at[c, pl.ds((1 - b_pos[s]) * SUB, SUB)], yr.at[c], 3, p, s, b_dev[s])
+
+    def sub_rows(p, s):
+        return pl.ds(base(p, s) + a_pos[s] * HALF + z * PIECE + b_pos[s] * SUB, SUB)
+
+    def last_back(p, s):
+        c = 2 * p + s
+        return remote(fb.at[c, pl.ds(b_pos[s] * SUB, SUB)], out_ref.at[sub_rows(p, s)], 4, p, s, b_dev[s])
+
+    def keep(p, s):
+        c = 2 * p + s
+        return pltpu.make_async_copy(fb.at[c, pl.ds(b_pos[s] * SUB, SUB)], out_ref.at[sub_rows(p, s)], loc.at[1, s, lax.rem(p, NS)])
+
+    def piece_of(p, s, k):
+        return out_ref.at[pl.ds(base(p, s) + a_pos[s] * HALF + k * PIECE, PIECE)]
+
+    def up_back(p, s, hop):
+        k = jnp.maximum(z - hop, 0)
+        return remote(piece_of(p, s, k), piece_of(p, s, k), 5 + hop, p, s, up_dev)
+
+    def down_back(p, s, hop):
+        k = jnp.minimum(z + hop, 3)
+        return remote(piece_of(p, s, k), piece_of(p, s, k), 8 + hop, p, s, down_dev)
+
+    def first_back(p, s):
+        rows = out_ref.at[pl.ds(base(p, s) + a_pos[s] * HALF, HALF)]
+        return remote(rows, rows, 11, p, s, a_dev[s])
+
+    def add(*terms):
+        total = terms[0].astype(jnp.float32)
+        for term in terms[1:]:
+            total = total + term.astype(jnp.float32)
+        return total.astype(jnp.bfloat16)
+
+    def step_a(p):
+        for s in range(2):
+            first(p, s).start()
+            mine(p, s).start()
+
+    def step_b(p):
+        for s in range(2):
+            c = 2 * p + s
+            first(p, s).wait_recv()
+            mine(p, s).wait()
+            xr[c] = add(own[c], xr[c])
+
+            @pl.when(z == 0)
+            def _():
+                up(p, s, 1).start()
+
+            @pl.when(z == 3)
+            def _():
+                down(p, s, 3).start()
+
+    def step_c(p):
+        for s in range(2):
+            c = 2 * p + s
+
+            @pl.when(z == 1)
+            def _():
+                up(p, s, 1).wait_recv()
+                ur[c, 2 * PIECE:] = add(ur[c, 2 * PIECE:], xr[c, 2 * PIECE:])
+                up(p, s, 2).start()
+
+            @pl.when(z == 2)
+            def _():
+                down(p, s, 3).wait_recv()
+                dr[c, : 2 * PIECE] = add(dr[c, : 2 * PIECE], xr[c, : 2 * PIECE])
+                down(p, s, 2).start()
+
+    def step_d(p):
+        for s in range(2):
+            c = 2 * p + s
+
+            @pl.when(z == 2)
+            def _():
+                up(p, s, 2).wait_recv()
+                ur[c, 3 * PIECE:] = add(ur[c, 3 * PIECE:], xr[c, 3 * PIECE:])
+                up(p, s, 3).start()
+
+            @pl.when(z == 1)
+            def _():
+                down(p, s, 2).wait_recv()
+                dr[c, :PIECE] = add(dr[c, :PIECE], xr[c, :PIECE])
+                down(p, s, 1).start()
+
+    def step_e(p):
+        for s in range(2):
+            c = 2 * p + s
+
+            @pl.when(z == 0)
+            def _():
+                down(p, s, 1).wait_recv()
+                fb[c] = add(xr[c, :PIECE], dr[c, :PIECE])
+
+            @pl.when(z == 1)
+            def _():
+                fb[c] = add(xr[c, PIECE: 2 * PIECE], ur[c, PIECE: 2 * PIECE], dr[c, PIECE: 2 * PIECE])
+
+            @pl.when(z == 2)
+            def _():
+                fb[c] = add(xr[c, 2 * PIECE: 3 * PIECE], ur[c, 2 * PIECE: 3 * PIECE], dr[c, 2 * PIECE: 3 * PIECE])
+
+            @pl.when(z == 3)
+            def _():
+                up(p, s, 3).wait_recv()
+                fb[c] = add(xr[c, 3 * PIECE:], ur[c, 3 * PIECE:])
+
+            last(p, s).start()
+
+    def step_f(p):
+        for s in range(2):
+            c = 2 * p + s
+            last(p, s).wait_recv()
+            rows = pl.ds(pl.multiple_of(b_pos[s] * SUB, SUB), SUB)
+            fb[c, rows] = add(fb[c, rows], yr[c])
+            last_back(p, s).start()
+            keep(p, s).start()
+
+    def step_g(p):
+        for s in range(2):
+            last_back(p, s).wait_recv()
+            keep(p, s).wait()
+
+            @pl.when(has_up)
+            def _():
+                up_back(p, s, 0).start()
+
+            @pl.when(has_down)
+            def _():
+                down_back(p, s, 0).start()
+
+    def step_h(p):
+        for s in range(2):
+            @pl.when(has_down)
+            def _():
+                up_back(p, s, 0).wait_recv()
+
+            @pl.when(has_down & has_up)
+            def _():
+                up_back(p, s, 1).start()
+
+            @pl.when(has_up)
+            def _():
+                down_back(p, s, 0).wait_recv()
+
+            @pl.when(has_down & has_up)
+            def _():
+                down_back(p, s, 1).start()
+
+    def step_i(p):
+        for s in range(2):
+            @pl.when(z >= 2)
+            def _():
+                up_back(p, s, 1).wait_recv()
+
+            @pl.when(z == 2)
+            def _():
+                up_back(p, s, 2).start()
+
+            @pl.when(z <= 1)
+            def _():
+                down_back(p, s, 1).wait_recv()
+
+            @pl.when(z == 1)
+            def _():
+                down_back(p, s, 2).start()
+
+    def step_j(p):
+        for s in range(2):
+            @pl.when(z == 3)
+            def _():
+                up_back(p, s, 2).wait_recv()
+
+            @pl.when(z == 0)
+            def _():
+                down_back(p, s, 2).wait_recv()
+
+            first_back(p, s).start()
+
+    def step_k(p):
+        for s in range(2):
+            first_back(p, s).wait()
+            first(p, s).wait_send()
+            last(p, s).wait_send()
+            last_back(p, s).wait_send()
+            for k in range(3):
+                @pl.when(z == k)
+                def _():
+                    up(p, s, k + 1).wait_send()
+
+                @pl.when(z == k + 1)
+                def _():
+                    down(p, s, k + 1).wait_send()
+
+            @pl.when(has_up)
+            def _():
+                up_back(p, s, 0).wait_send()
+
+            @pl.when(has_down)
+            def _():
+                down_back(p, s, 0).wait_send()
+
+            @pl.when(has_up & has_down)
+            def _():
+                up_back(p, s, 1).wait_send()
+                down_back(p, s, 1).wait_send()
+
+            @pl.when(z == 2)
+            def _():
+                up_back(p, s, 2).wait_send()
+
+            @pl.when(z == 1)
+            def _():
+                down_back(p, s, 2).wait_send()
+
+    small_devs = (c_dev, x_dev, y_dev, z1_dev, z2_dev)
+
+    def small_copy(i):
+        return pltpu.make_async_remote_copy(
+            src_ref=sacc, dst_ref=sbuf.at[i], send_sem=ssend.at[i], recv_sem=srecv.at[i],
+            device_id=small_devs[i], device_id_type=MESH)
+
+    sacc[...] = small_ref[...]
+    small_copy(0).start()
+    for q in range(AHEAD):
+        step_a(q)
+
+    def iteration(t, _):
+        def run(step, offset):
+            p = t - offset
+
+            @pl.when((p >= 0) & (p < pairs))
+            def _():
+                step(p)
+
+        steps = dict(a=step_a, b=step_b, c=step_c, d=step_d, e=step_e, f=step_f, g=step_g, h=step_h, i=step_i, j=step_j, k=step_k)
+        for name, off in ORDER:
+            run(steps[name], off)
+        for i in range(5):
+            @pl.when(t == i + 1)
+            def _():
+                small_copy(i).wait()
+                sacc[...] += sbuf[i]
+                if i < 4:
+                    small_copy(i + 1).start()
+        return 0
+
+
+    lax.fori_loop(0, pairs + max(o for _, o in ORDER), iteration, 0)
+    small_out[...] = sacc[...]
+
+
+def reduce_all(grads, small):
+    rows = grads.shape[0]
+    chunks = rows // CH
+    return pl.pallas_call(
+        functools.partial(reduce_kernel, chunks // 2),
+        out_shape=(jax.ShapeDtypeStruct(grads.shape, jnp.bfloat16), jax.ShapeDtypeStruct(small.shape, jnp.float32)),
+        in_specs=[pl.BlockSpec(memory_space=pl.ANY), pl.BlockSpec(memory_space=pltpu.VMEM)],
+        out_specs=(pl.BlockSpec(memory_space=pl.ANY), pl.BlockSpec(memory_space=pltpu.VMEM)),
+        scratch_shapes=[
+            pltpu.VMEM((chunks, HALF, 1024), jnp.bfloat16),
+            pltpu.VMEM((chunks, HALF, 1024), jnp.bfloat16),
+            pltpu.VMEM((chunks, HALF, 1024), jnp.bfloat16),
+            pltpu.VMEM((chunks, HALF, 1024), jnp.bfloat16),
+            pltpu.VMEM((chunks, PIECE, 1024), jnp.bfloat16),
+            pltpu.VMEM((chunks, SUB, 1024), jnp.bfloat16),
+            pltpu.VMEM((SMALL, 1024), jnp.float32),
+            pltpu.VMEM((5, SMALL, 1024), jnp.float32),
+            pltpu.SemaphoreType.DMA((12, 2, NS)),
+            pltpu.SemaphoreType.DMA((12, 2, NS)),
+            pltpu.SemaphoreType.DMA((2, 2, NS)),
+            pltpu.SemaphoreType.DMA((5,)),
+            pltpu.SemaphoreType.DMA((5,)),
+        ],
+        compiler_params=pltpu.CompilerParams(collective_id=0, has_side_effects=True, vmem_limit_bytes=56 << 20),
+    )(grads, small)
 
 
 epsilon = 1e-05
@@ -81,6 +439,22 @@
         "ghsk,gshe->gkhe", grad_score, query_blk, preferred_element_type=jnp.float32
     )
     return (grad_query, grad_key, grad_value)
+
+
+def fold(matrix):
+    rows, width = matrix.shape
+    if width < 1024:
+        return jnp.concatenate(jnp.split(matrix, 1024 // width, axis=0), axis=1)
+    return jnp.concatenate(jnp.split(matrix, width // 1024, axis=1), axis=0)
+
+
+def unfold(block, rows):
+    height = block.shape[0]
+    if height < rows:
+        pieces = jnp.split(block, rows // height, axis=1)
+        return jnp.concatenate(pieces, axis=0).astype(jnp.float32)
+    pieces = jnp.split(block, height // rows, axis=0)
+    return jnp.concatenate(pieces, axis=1).astype(jnp.float32)
 
 
 def pair_apply(block_fn, span, operands):
@@ -268,6 +642,47 @@
     grad_inputs, grad_gain_input, grad_shift_input = norm_back(
         input_rows, gain_input, shift_input, grad_input_normed
     )
+    core = lax.axis_index("mp")
+    half = mlp_in_bias.shape[0]
+    bias_row = jnp.zeros((2, half), jnp.float32).at[core].set(grad_mlp_in_bias)
+    out_bias = jnp.sum(cotangent, axis=0, dtype=jnp.float32)
+    small = jnp.concatenate(
+        [
+            jnp.stack(
+                [
+                    grad_gain_latent,
+                    grad_shift_latent,
+                    grad_gain_input,
+                    grad_shift_input,
+                    grad_gain_self,
+                    grad_shift_self,
+                    grad_gain_mlp,
+                    grad_shift_mlp,
+                    out_bias,
+                ]
+            ),
+            bias_row.reshape(4, 1024),
+            jnp.zeros((3, 1024), jnp.float32),
+        ]
+    )
+    tall = (grad_cross_query, grad_cross_key, grad_cross_value, grad_self_query, grad_self_key, grad_self_value)
+    blocks = [grad_mlp_out, fold(grad_mlp_in), grad_self_out, grad_cross_out] + [fold(v) for v in tall]
+    packed = jnp.concatenate([v.astype(jnp.bfloat16) for v in blocks])
+    if lax.axis_size("dp") == 16:
+        packed, small = reduce_all(packed, small)
+    else:
+        packed, small = lax.psum(packed, "dp"), lax.psum(small, ("dp", "mp"))
+    parts, place = [], 0
+    for block in blocks:
+        parts.append(lax.slice_in_dim(packed, place, place + block.shape[0]))
+        place += block.shape[0]
+    grad_mlp_out = parts[0].astype(jnp.float32)
+    grad_mlp_in = unfold(parts[1], 1024)
+    grad_self_out = parts[2].astype(jnp.float32)
+    grad_cross_out = parts[3].astype(jnp.float32)
+    grad_cross_query, grad_cross_key, grad_cross_value, grad_self_query, grad_self_key, grad_self_value = [
+        unfold(v, 1024) for v in parts[4:]
+    ]
     (
         grad_gain_latent,
         grad_shift_latent,
@@ -277,49 +692,9 @@
         grad_shift_self,
         grad_gain_mlp,
         grad_shift_mlp,
-    ) = lax.psum(
-        (
-            grad_gain_latent,
-            grad_shift_latent,
-            grad_gain_input,
-            grad_shift_input,
-            grad_gain_self,
-            grad_shift_self,
-            grad_gain_mlp,
-            grad_shift_mlp,
-        ),
-        ("dp", "mp"),
-    )
-    (
-        grad_cross_query,
-        grad_cross_key,
-        grad_cross_value,
-        grad_cross_out,
-        grad_self_query,
-        grad_self_key,
-        grad_self_value,
-        grad_self_out,
-        grad_mlp_in,
-        grad_mlp_in_bias,
-        grad_mlp_out,
         grad_mlp_out_bias,
-    ) = lax.psum(
-        (
-            grad_cross_query,
-            grad_cross_key,
-            grad_cross_value,
-            grad_cross_out,
-            grad_self_query,
-            grad_self_key,
-            grad_self_value,
-            grad_self_out,
-            grad_mlp_in,
-            grad_mlp_in_bias,
-            grad_mlp_out,
-            grad_mlp_out_bias,
-        ),
-        "dp",
-    )
+    ) = [small[i] for i in range(9)]
+    grad_mlp_in_bias = lax.dynamic_slice_in_dim(small[9:13].reshape(-1), core * half, half)
     return (
         result_latents,
         grad_latents,

time: 1510 us -> 851 us (0.56)
  waiting for transfers between devices: 881 us -> 105 us
  Pallas kernels: 0 us -> 247 us
  blocking collectives: 123 us -> 0 us
  other arithmetic: 72 us -> 96.3 us
    psum x1 -> x0, waiting for transfers between devices: 774 us -> none  [local(): lax.psum((grad_cross_query, grad_cross_key, grad_cross_value, grad_cross_...]
    pallas_call x0 -> x1, Pallas kernels: none -> 247 us  [reduce_all(): pl.pallas_call(functools.partial(reduce_kernel, chunks // 2), out_shape=(...]
    psum x2 -> x0, blocking collectives: 123 us -> none  [the longest x1 80.9 us: local(): lax.psum((grad_cross_query, grad_cross_key, grad_cross_value, grad_cross_...]
    convert_element_type x0 -> x6, other arithmetic: none -> 21.5 us  [the longest x3 7.79 us: unfold(): return jnp.concatenate(pieces, axis=0).astype(jnp.float32)]
    unnamed x190 -> x166, local copies, waits for them, and re-layouts: 33.5 us -> 17 us
  transfers between devices with their start and end apart: 15 -> 14, of which waited for: 13 -> 12; matrix products, arithmetic and copies ran while one was open for 12% -> 19% of each run, Pallas kernels for 0% -> 0%
where the time goes in v1:
time: 851 us; the launch traced here: 845 us
  matrix products  324 us (38%)
  Pallas kernels  247 us (29%)
  waiting for transfers between devices  105 us (12%)
  other arithmetic  96.3 us (11%)
  local copies, waits for them, and re-layouts  56 us (7%)
  between operations  15.5 us (2%)
    pallas_call x1, Pallas kernels, reduce_all(): pl.pallas_call(functools.partial(reduce_kernel, chunks // 2), out_shape=(...  247 us
    dot_general x2, matrix products, attend_back(): jnp.einsum('ghsk,gshe->gkhe', grad_score, query_blk, preferred_element_ty...  85.8 us
    dot_general x2, matrix products, attend_back(): jnp.einsum('ghsk,gkhe->gshe', grad_score, key_blk, preferred_element_type...  69 us
    dot_general x10, matrix products, contract_cols(): lax.dot_general(left, right, (((1,), (1,)), ((), ())), preferred_element_...  37 us
    dot_general x10, matrix products, product(): return jnp.dot(left, right, preferred_element_type=jnp.float32)  36.1 us
    dot_general x2, matrix products, attend_back(): jnp.einsum('ghsk,gshe->gkhe', attn_prob, grad_blk, preferred_element_type...  21.1 us
    dot_general x10, matrix products, contract_rows(): lax.dot_general(left, right, (((0,), (0,)), ((), ())), preferred_element_...  20.1 us
    dot_general x2, matrix products, attend_back(): jnp.einsum('gshe,gkhe->ghsk', grad_blk, value_blk, preferred_element_type...  19.4 us
  transfers between devices with their start and end apart: 14, of which 12 were waited for; matrix products, arithmetic and copies ran while one was open for 19% of the time, Pallas kernels for 0%

profile of v1, /device:TPU:0, one launch (start us, length us, event | category | flops | bytes accessed | tf_op | source)
XLA Modules:
  0.0 845.0 jit_solution(1719755534116031452)
XLA Ops:
  19.5 5.7 all-gather.10.cloned.1.call-done
  28.5 13.6 %all-gather.8.cloned.1.call-done = bf16[2048,1024]{1,0:T(8,128)(2,1)} async-done(((bf16[1024,1024]{1,0:T(8,128)(2,1)}), bf16[2048,1024]{1,0:T(8,128)(2,1)}) %all-gather.8.cloned.1.call-update) | async-done | bytes 4194320 | tf_op jit(solution)/shard_map/all_gather | solution.py:542
  42.1 4.8 convolution_convert_fusion.2
  52.9 6.6 convolution_convert_fusion.1
  63.4 4.5 squeeze.93
  67.8 15.3 %fusion.5 = (f32[2,16,256]{2,1,0:T(8,128)S(1)}, f32[2,16,256,1024]{3,2,1,0:T(8,128)}) fusion(pred[2,1024]{1,0:T(4,128)(4,1)S(1)} %iota_compare_fusion, bf16[2,1024,16,32]{1,0,3,2:T(2,128)(2,1)} %squeeze.93, bf16[2,256,16,32]{1,0,3,2:T(2,128)(2,1)} %squeeze.92), kind=kOutput, calls=%fused_computation.8 | convolution fusion | flops 562028544 | bytes 36210688 | tf_op jit(solution)/shard_map/while/body/eval_jaxpr/gshe,gkhe->ghsk/dot_general | solution.py:404
  83.2 14.7 %exponential_reduce_fusion = f32[2,16,256]{2,1,0:T(8,128)S(1)} fusion(f32[2,16,256,1024]{3,2,1,0:T(8,128)} %get-tuple-element.199, f32[2,16,256]{2,1,0:T(8,128)S(1)} %get-tuple-element.198, pred[2,1024]{1,0:T(4,128)(4,1)S(1)} %iota_compare_fusion), kind=kLoop, calls=%fused_computation.6 | loop fusion | flops 33546240 | bytes 33622016 | tf_op jit(solution)/shard_map/while/body/eval_jaxpr/reduce_sum | solution.py:415
  97.9 15.2 %fusion.119 = bf16[2,256,16,32]{1,3,2,0:T(8,128)(2,1)} fusion(bf16[2,1024,16,32]{1,0,3,2:T(2,128)(2,1)S(1)} %squeeze.91, f32[2,16,256,1024]{3,2,1,0:T(8,128)} %get-tuple-element.199, f32[2,16,256]{2,1,0:T(8,128)S(1)} %log_add_fusion.1, pred[2,1024]{1,0:T(4,128)(4,1)S(1)} %iota_compare_fusion), kind=kOutput, calls=%fused_computation.151 | convolution fusion | flops 570687488 | bytes 36210688 | tf_op jit(solution)/shard_map/while/body/eval_jaxpr/ghsk,gkhe->gshe/dot_general | solution.py:418
  118.7 9.8 %reduce-scatter.8.cloned.1.call-done = bf16[256,1024]{1,0:T(8,128)(2,1)} async-done(((bf16[512,1024]{1,0:T(8,128)(2,1)}), bf16[256,1024]{1,0:T(8,128)(2,1)}) %reduce-scatter.8.cloned.1.call-update) | async-done | bytes 524304 | tf_op jit(solution)/shard_map/reduce_scatter | solution.py:551
  133.4 10.3 %all-gather.12.cloned.1.call-done = bf16[512,1024]{1,0:T(8,128)(2,1)} async-done(((bf16[256,1024]{1,0:T(8,128)(2,1)}), bf16[512,1024]{1,0:T(8,128)(2,1)}) %all-gather.12.cloned.1.call-update) | async-done | bytes 1048592 | tf_op jit(solution)/shard_map/all_gather | solution.py:555
  164.9 9.8 %reduce-scatter.10.cloned.1.call-done = bf16[256,1024]{1,0:T(8,128)(2,1)} async-done(((bf16[512,1024]{1,0:T(8,128)(2,1)}), bf16[256,1024]{1,0:T(8,128)(2,1)}) %reduce-scatter.10.cloned.1.call-update) | async-done | bytes 524304 | tf_op jit(solution)/shard_map/reduce_scatter | solution.py:563
  178.4 9.4 %all-gather.14.cloned.1.call-done = bf16[512,1024]{1,0:T(8,128)(2,1)} async-done(((bf16[256,1024]{1,0:T(8,128)(2,1)}), bf16[512,1024]{1,0:T(8,128)(2,1)}) %all-gather.14.cloned.1.call-update) | async-done | bytes 1048592 | tf_op jit(solution)/shard_map/all_gather | solution.py:567
  187.8 6.9 fusion.200
  194.6 4.9 all-gather.16.cloned.1.call-done
  199.6 15.9 %convert_reduce_fusion.2 = (f32[2048]{0:T(1024)S(1)}, bf16[512,2048]{1,0:T(8,128)(2,1)S(1)}, f32[512,2048]{1,0:T(8,128)}) fusion(f32[512,2048]{1,0:T(8,128)} %fusion.200, f32[2048]{0:T(1024)S(1)} %copy-done.59, bf16[512,1024]{1,0:T(8,128)(2,1)} %all-gather.16.cloned.1.call-done, bf16[2048,1024]{1,0:T(8,128)(2,1)} %param.48), kind=kOutput, calls=%fused_computation.51 | convolution fusion | flops 2226124800 | bytes 15745024 | tf_op jit(solution)/shard_map/dot_general | solution.py:398
  220.2 4.6 multiply_convert_fusion.2
  231.4 11.2 %reduce-scatter.12.cloned.1.call-done = bf16[256,1024]{1,0:T(8,128)(2,1)} async-done(((bf16[512,1024]{1,0:T(8,128)(2,1)}), bf16[256,1024]{1,0:T(8,128)(2,1)}) %reduce-scatter.12.cloned.1.call-update) | async-done | bytes 524304 | tf_op jit(solution)/shard_map/reduce_scatter | solution.py:571
  248.1 10.3 %all-gather.18.cloned.1.call-done = bf16[512,1024]{1,0:T(8,128)(2,1)} async-done(((bf16[256,1024]{1,0:T(8,128)(2,1)}), bf16[512,1024]{1,0:T(8,128)(2,1)}) %all-gather.18.cloned.1.call-update) | async-done | bytes 1048592 | tf_op jit(solution)/shard_map/all_gather | solution.py:594
  262.9 4.7 fusion.139
  267.6 14.5 %fusion.109 = bf16[2,256,16,32]{1,3,2,0:T(8,128)(2,1)} fusion(f32[2,16,256,256]{2,3,1,0:T(8,128)} %fusion.139, f32[2,16,256,256]{2,3,1,0:T(8,128)} %copy-done.4, f32[2,16,256]{2,1,0:T(8,128)S(1)} %log_add_fusion, pred[2,256]{1,0:T(4,128)(4,1)S(1)} %iota_compare_fusion.1, bf16[2,256,16,32]{1,0,3,2:T(2,128)(2,1)} %copy-done.29), kind=kOutput, calls=%fused_computation.147 | convolution fusion | flops 157556992 | bytes 17859072 | tf_op jit(solution)/shard_map/while/body/eval_jaxpr/ghsk,gkhe->gshe/dot_general | solution.py:435
  282.1 16.3 %fusion.106 = bf16[2,256,16,32]{1,3,2,0:T(8,128)(2,1)} fusion(f32[2,16,256,256]{2,3,1,0:T(8,128)} %fusion.139, f32[2,16,256,256]{2,3,1,0:T(8,128)} %copy-done.4, f32[2,16,256]{2,1,0:T(8,128)S(1)} %log_add_fusion, pred[2,256]{1,0:T(4,128)(4,1)S(1)} %iota_compare_fusion.1, bf16[2,256,16,32]{1,0,3,2:T(2,128)(2,1)S(1)} %copy-done.30), kind=kOutput, calls=%fused_computation.146 | convolution fusion | flops 157556992 | bytes 17859072 | tf_op jit(solution)/shard_map/while/body/eval_jaxpr/ghsk,gshe->gkhe/dot_general | solution.py:438
  298.4 5.3 fusion.113
  310.1 9.6 %reduce-scatter.16.cloned.1.call-done = bf16[256,1024]{1,0:T(8,128)(2,1)} async-done(((bf16[512,1024]{1,0:T(8,128)(2,1)}), bf16[256,1024]{1,0:T(8,128)(2,1)}) %reduce-scatter.16.cloned.1.call-update) | async-done | bytes 524304 | tf_op jit(solution)/shard_map/reduce_scatter | solution.py:603
  326.7 9.6 %all-gather.20.cloned.1.call-done = bf16[512,1024]{1,0:T(8,128)(2,1)} async-done(((bf16[256,1024]{1,0:T(8,128)(2,1)}), bf16[512,1024]{1,0:T(8,128)(2,1)}) %all-gather.20.cloned.1.call-update) | async-done | bytes 1048592 | tf_op jit(solution)/shard_map/all_gather | solution.py:617
  338.9 14.7 %fusion.74 = f32[2,16,256,1024]{3,2,1,0:T(8,128)} fusion(bf16[2,1024,16,32]{1,0,3,2:T(2,128)(2,1)} %copy-done.10, bf16[2,256,16,32]{1,0,3,2:T(2,128)(2,1)S(1)} %squeeze.98), kind=kOutput, calls=%fused_computation.86 | convolution fusion | flops 536870912 | bytes 36175872 | tf_op jit(solution)/shard_map/while/body/eval_jaxpr/gshe,gkhe->ghsk/dot_general | solution.py:430
  353.6 54.5 %fusion.114 = bf16[2,256,16,32]{1,3,2,0:T(8,128)(2,1)S(1)} fusion(f32[2,16,256,1024]{3,2,1,0:T(8,128)} %fusion.74, f32[2,16,256,1024]{3,2,1,0:T(8,128)} %get-tuple-element.199, f32[2,16,256]{2,1,0:T(8,128)S(1)} %log_add_fusion.1, pred[2,1024]{1,0:T(4,128)(4,1)S(1)} %iota_compare_fusion, bf16[2,1024,16,32]{1,0,3,2:T(2,128)(2,1)} %squeeze.93), kind=kOutput, calls=%fused_computation.150 | convolution fusion | flops 629416960 | bytes 69765120 | tf_op jit(solution)/shard_map/while/body/eval_jaxpr/ghsk,gkhe->gshe/dot_general | solution.py:435
  411.8 15.8 %convert_bitcast_fusion = bf16[2,1024,16,32]{1,3,2,0:T(8,128)(2,1)} fusion(bf16[2,256,16,32]{1,0,3,2:T(2,128)(2,1)S(1)} %squeeze.98, f32[2,16,256,1024]{3,2,1,0:T(8,128)} %get-tuple-element.199, f32[2,16,256]{2,1,0:T(8,128)S(1)} %log_add_fusion.1, pred[2,1024]{1,0:T(4,128)(4,1)S(1)} %iota_compare_fusion), kind=kOutput, calls=%fused_computation.83 | convolution fusion | flops 571473920 | bytes 36210688 | tf_op jit(solution)/shard_map/while/body/eval_jaxpr/ghsk,gshe->gkhe/dot_general | solution.py:427
  427.7 69.6 %convert_bitcast_fusion.1 = bf16[2,1024,16,32]{1,3,2,0:T(8,128)(2,1)} fusion(f32[2,16,256,1024]{3,2,1,0:T(8,128)} %fusion.74, f32[2,16,256,1024]{3,2,1,0:T(8,128)} %get-tuple-element.199, f32[2,16,256]{2,1,0:T(8,128)S(1)} %log_add_fusion.1, pred[2,1024]{1,0:T(4,128)(4,1)S(1)} %iota_compare_fusion, bf16[2,256,16,32]{1,0,3,2:T(2,128)(2,1)S(1)} %copy-done.12), kind=kOutput, calls=%fused_computation.84 | convolution fusion | flops 630203392 | bytes 69765120 | tf_op jit(solution)/shard_map/while/body/eval_jaxpr/ghsk,gshe->gkhe/dot_general | solution.py:438
  507.0 4.6 add_convert_fusion
  512.6 4.4 convolution_convert_fusion
  559.7 247.0 %shard_map.407 = (bf16[8192,1024]{1,0:T(8,128)(2,1)}, f32[16,1024]{1,0:T(8,128)}) custom-call(bf16[8192,1024]{1,0:T(8,128)(2,1)} %maximum_dynamic-update-slice_fusion.g_ref, f32[16,1024]{1,0:T(8,128)} %concatenate.66.small_ref), custom_call_target="tpu_custom_call" | custom-call | tf_op jit(solution)/shard_map/pallas_call | solution.py:347
  810.9 4.8 slice_convert_fusion.1
  (319 shorter events, 180.7 us)
Async XLA Ops:
  7.2 45.6 %copy-start = (bf16[1024,512]{1,0:T(8,128)(2,1)S(1)}, bf16[1024,512]{1,0:T(8,128)(2,1)}, u32[]{:S(2)}) copy-start(bf16[1024,512]{1,0:T(8,128)(2,1)} %param.35) | copy-start | bytes 3145732
  7.2 17.9 %all-gather.10.cloned.1.call-start = ((), (), s32[]{:S(2)}) async-start(), calls=%async_computation.8 | async-start | bytes 1572864 | tf_op jit(solution)/shard_map/all_gather | solution.py:541
  13.3 28.9 %all-gather.8.cloned.1.call-start = ((), (), s32[]{:S(2)}) async-start(), calls=%async_computation.7 | async-start | bytes 6291456 | tf_op jit(solution)/shard_map/all_gather | solution.py:542
  19.4 109.2 %reduce-scatter.8.cloned.1.call-start = ((), (), s32[]{:S(2)}) async-start(), calls=%async_computation.9 | async-start | bytes 1572864 | tf_op jit(solution)/shard_map/reduce_scatter | solution.py:551
  52.8 45.1 %copy-start.10 = (bf16[2,1024,16,32]{1,0,3,2:T(2,128)(2,1)}, bf16[2,1024,16,32]{1,0,3,2:T(2,128)(2,1)S(1)}, u32[]{:S(2)}) copy-start(bf16[2,1024,16,32]{1,0,3,2:T(2,128)(2,1)S(1)} %squeeze.91) | copy-start | bytes 6291460
  113.1 15.4 %copy-start.1 = (bf16[256,1024]{1,0:T(8,128)(2,1)S(1)}, bf16[256,1024]{1,0:T(8,128)(2,1)}, u32[]{:S(2)}) copy-start(bf16[256,1024]{1,0:T(8,128)(2,1)} %param.26) | copy-start | bytes 1572868
  113.1 18.0 %copy-start.43 = (f32[1024]{0:T(1024)S(1)}, f32[1024]{0:T(1024)}, u32[]{:S(2)}) copy-start(f32[1024]{0:T(1024)} %param.38) | copy-start | bytes 12292
  113.2 18.0 %copy-start.60 = (f32[1024]{0:T(1024)S(1)}, f32[1024]{0:T(1024)}, u32[]{:S(2)}) copy-start(f32[1024]{0:T(1024)} %param.39) | copy-start | bytes 12292
  114.9 28.7 %copy-start.33 = (bf16[1024,512]{1,0:T(8,128)(2,1)S(1)}, bf16[1024,512]{1,0:T(8,128)(2,1)}, u32[]{:S(2)}) copy-start(bf16[1024,512]{1,0:T(8,128)(2,1)} %param.42) | copy-start | bytes 3145732
  118.7 25.0 %all-gather.12.cloned.1.call-start = ((), (), s32[]{:S(2)}) async-start(), calls=%async_computation.10 | async-start | bytes 1572864 | tf_op jit(solution)/shard_map/all_gather | solution.py:555
  133.3 41.4 %reduce-scatter.10.cloned.1.call-start = ((), (), s32[]{:S(2)}) async-start(), calls=%async_computation.11 | async-start | bytes 1572864 | tf_op jit(solution)/shard_map/reduce_scatter | solution.py:563
  145.9 13.3 %copy-start.18 = (bf16[2,256,16,32]{1,0,3,2:T(2,128)(2,1)}, bf16[2,256,16,32]{1,0,3,2:T(2,128)(2,1)S(1)}, u32[]{:S(2)}) copy-start(bf16[2,256,16,32]{1,0,3,2:T(2,128)(2,1)S(1)} %squeeze.94) | copy-start | bytes 1572868
  162.5 12.3 %copy-start.5 = (bf16[256,1024]{1,0:T(8,128)(2,1)S(1)}, bf16[256,1024]{1,0:T(8,128)(2,1)}, u32[]{:S(2)}) copy-start(bf16[256,1024]{1,0:T(8,128)(2,1)} %reduce-scatter.8.cloned.1.call-done) | copy-start | bytes 1572868
  163.0 13.3 %copy-start.52 = (f32[1024]{0:T(1024)S(1)}, f32[1024]{0:T(1024)}, u32[]{:S(2)}) copy-start(f32[1024]{0:T(1024)} %param.44) | copy-start | bytes 12292
  163.0 13.3 %copy-start.61 = (f32[1024]{0:T(1024)S(1)}, f32[1024]{0:T(1024)}, u32[]{:S(2)}) copy-start(f32[1024]{0:T(1024)} %param.45) | copy-start | bytes 12292
  164.9 22.9 %all-gather.14.cloned.1.call-start = ((), (), s32[]{:S(2)}) async-start(), calls=%async_computation.12 | async-start | bytes 1572864 | tf_op jit(solution)/shard_map/all_gather | solution.py:567
  177.4 22.1 %all-gather.16.cloned.1.call-start = ((), (), s32[]{:S(2)}) async-start(), calls=%async_computation.14 | async-start | bytes 1572864 | tf_op jit(solution)/shard_map/all_gather | solution.py:543
  178.2 21.4 %copy-start.59 = (f32[2048]{0:T(1024)S(1)}, f32[2048]{0:T(1024)}, u32[]{:S(2)}) copy-start(f32[2048]{0:T(1024)} %param.47) | copy-start | bytes 24580
  178.2 51.8 %reduce-scatter.14.cloned.1.call-start = ((), (), s32[]{:S(2)}) async-start(), calls=%async_computation.15 | async-start | bytes 1572864 | tf_op jit(solution)/shard_map/reduce_scatter | solution.py:584
  199.6 17.2 %copy-start.66 = (bf16[1024,2048]{1,0:T(8,128)(2,1)S(1)}, bf16[1024,2048]{1,0:T(8,128)(2,1)}, u32[]{:S(2)}) copy-start(bf16[1024,2048]{1,0:T(8,128)(2,1)} %param.46) | copy-start | bytes 12582916
  220.1 22.5 %reduce-scatter.12.cloned.1.call-start = ((), (), s32[]{:S(2)}) async-start(), calls=%async_computation.13 | async-start | bytes 1572864 | tf_op jit(solution)/shard_map/reduce_scatter | solution.py:571
  226.1 16.5 %copy-start.63 = (f32[1024]{0:T(1024)S(1)}, f32[1024]{0:T(1024)}, u32[]{:S(2)}) copy-start(f32[1024]{0:T(1024)} %param.49) | copy-start | bytes 12292
  229.5 29.0 %all-gather.18.cloned.1.call-start = ((), (), s32[]{:S(2)}) async-start(), calls=%async_computation.16 | async-start | bytes 1572864 | tf_op jit(solution)/shard_map/all_gather | solution.py:594
  245.1 17.8 %copy-start.19 = (bf16[2,256,16,32]{1,0,3,2:T(2,128)(2,1)S(1)}, bf16[2,256,16,32]{1,0,3,2:T(2,128)(2,1)}, u32[]{:S(2)}) copy-start(bf16[2,256,16,32]{1,0,3,2:T(2,128)(2,1)} %copy-done.18) | copy-start | bytes 1572868
  248.1 71.6 %reduce-scatter.16.cloned.1.call-start = ((), (), s32[]{:S(2)}) async-start(), calls=%async_computation.17 | async-start | bytes 1572864 | tf_op jit(solution)/shard_map/reduce_scatter | solution.py:603
  267.6 14.5 %copy-start.30 = (bf16[2,256,16,32]{1,0,3,2:T(2,128)(2,1)S(1)}, bf16[2,256,16,32]{1,0,3,2:T(2,128)(2,1)}, u32[]{:S(2)}) copy-start(bf16[2,256,16,32]{1,0,3,2:T(2,128)(2,1)} %squeeze.95) | copy-start | bytes 1572868
  308.1 14.8 %copy-start.9 = (f32[256,1024]{1,0:T(8,128)S(1)}, f32[256,1024]{1,0:T(8,128)}, u32[]{:S(2)}) copy-start(f32[256,1024]{1,0:T(8,128)} %copy-done.8) | copy-start | bytes 3145732
  309.9 16.1 %copy-start.65 = (s32[2]{0:T(128)S(1)}, s32[2]{0:T(128)}, u32[]{:S(2)}) copy-start(s32[2]{0:T(128)} %constant.212.clone.1) | copy-start | bytes 28
  309.9 26.4 %all-gather.20.cloned.1.call-start = ((), (), s32[]{:S(2)}) async-start(), calls=%async_computation.18 | async-start | bytes 1572864 | tf_op jit(solution)/shard_map/all_gather | solution.py:617
  325.9 219.3 %reduce-scatter.18.cloned.1.call-start = ((), (), s32[]{:S(2)}) async-start(), calls=%async_computation.19 | async-start | bytes 1572864 | tf_op jit(solution)/shard_map/reduce_scatter | solution.py:631
  411.7 15.9 %copy-start.12 = (bf16[2,256,16,32]{1,0,3,2:T(2,128)(2,1)S(1)}, bf16[2,256,16,32]{1,0,3,2:T(2,128)(2,1)}, u32[]{:S(2)}) copy-start(bf16[2,256,16,32]{1,0,3,2:T(2,128)(2,1)} %squeeze.92) | copy-start | bytes 1572868
  411.8 139.0 %reduce-scatter.20.cloned.1.call-start = ((), (), s32[]{:S(2)}) async-start(), calls=%async_computation.20 | async-start | bytes 6291456 | tf_op jit(solution)/shard_map/reduce_scatter | solution.py:634
  (59 other events, 212.6 us)
Sparse Core Ops, SparseCore 0:
  13.4 11.7 all-gather.9
  27.3 14.8 all-gather.7
  118.8 9.6 reduce-scatter.7
  133.4 10.1 all-gather.11
  165.0 9.6 reduce-scatter.9
  177.5 10.1 all-gather.13
  189.3 10.1 all-gather.15
  220.2 9.6 reduce-scatter.13
  232.9 9.6 reduce-scatter.11
  248.2 10.1 all-gather.17
  310.0 9.6 reduce-scatter.15
  326.0 10.1 all-gather.19
  411.9 9.6 reduce-scatter.17
  511.7 13.2 reduce-scatter.19
